TPU v7x, 32 devices: a whole 2x2x4 slice. The times are simulated.
32 devices in a mesh: shell: 4 (over z), sky: 8 (over y, x, core).
Axes of the slice: x: 2, y: 2, z: 4, core: 2. Of those that a mesh axis runs over, the one named last changes fastest.
Arguments:
- density: bfloat16 [100, 384, 384], P('shell', 'sky'), may hold values from -6 to 6
- kernel_table: float32 [16, 4], replicated, may hold values from 0.02 to 0.4
- shell_row: int32 [100], P('shell'), may hold values from 0 to 15, as said below
- theta_first: bfloat16 [6, 4, 64], replicated, may hold values from -1.25 to 1.25
- bias_first: float32 [64], replicated, may hold values from -3 to 3
- theta_second: bfloat16 [6, 64, 64], replicated, may hold values from -0.3125 to 0.3125
- bias_second: float32 [64], replicated, may hold values from -3 to 3
Outputs:
- features: bfloat16 [64, 384, 384], P('shell', 'sky')
Inputs may be any that keep to these rules, and one draw needn't show every extreme that they name: `shell_row`: each shell names one row of kernel_table; both the first and the last row are named.
All inputs are finite; a program needn't handle non-finite values.
Results may differ from a plain program's by a relative error of at most 0.0062.
Values may be sent and summed in bfloat16 or wider, within the bound.
A program may use at most 128 MiB of HBM per device.

v0:
```python
import jax
import jax.numpy as jnp
from jax import lax
from jax.sharding import PartitionSpec as P


def padded(block, sides, width):
    for axis, dim in sides:
        count = lax.axis_size(axis)
        forward = [(i, i + 1) for i in range(count - 1)]
        forward.append((count - 1, 0))
        backward = [(target, source) for source, target in forward]
        low = lax.ppermute(
            lax.slice_in_dim(block, block.shape[dim] - width, None, axis=dim), axis, forward
        )
        high = lax.ppermute(lax.slice_in_dim(block, 0, width, axis=dim), axis, backward)
        block = jnp.concatenate([low, block, high], axis=dim)
    return block


def lateral(source_field):
    right_side = jnp.pad(source_field[:, :, 1:], ((0, 0), (0, 0), (0, 1)))
    left_side = jnp.pad(source_field[:, :, :-1], ((0, 0), (0, 0), (1, 0)))
    return right_side + left_side


def apply_rows(extended):
    return -0.25 * (extended[:, :-2] + extended[:, 2:] + lateral(extended[:, 1:-1]))


def basis_of(source_field, is_first, degrees):
    collected = [source_field.astype(jnp.bfloat16)]
    earlier = source_field.astype(jnp.float32)
    current = earlier
    for degree in range(1, degrees):
        if is_first:
            extended = padded(current, (("sky", 1),), 1)
        else:
            extended = padded(current, (("sky", 1),), 1)
        mapped = apply_rows(extended)
        if degree == 1:
            following = mapped
        else:
            following = 2.0 * mapped - earlier
        earlier = current
        current = following
        collected.append(following.astype(jnp.bfloat16))
    return jnp.stack(collected)


def per_device(
    density, kernel_table, shell_row, theta_first, bias_first, theta_second, bias_second
):
    degrees = theta_first.shape[0]
    table_rows = kernel_table.shape[0]
    table_ids = lax.broadcasted_iota(jnp.int32, (shell_row.shape[0], table_rows), 1)
    selector = (shell_row[:, None] == table_ids).astype(jnp.float32)
    weights = jnp.dot(selector, kernel_table, precision=lax.Precision.HIGHEST).astype(jnp.bfloat16)
    partial_sum = jnp.einsum("sb,syx->byx", weights, density, preferred_element_type=jnp.float32)
    convergence = lax.psum(partial_sum, "shell")
    first_basis = basis_of(convergence, True, degrees)
    groups = lax.axis_size("shell")
    shell_index = lax.axis_index("shell")
    width_out = theta_second.shape[2] // groups
    out_start = shell_index * width_out
    hidden = jnp.einsum(
        "kbo,kbyx->oyx", theta_first, first_basis, preferred_element_type=jnp.float32
    )
    hidden = jnp.maximum(hidden + bias_first[:, None, None], 0.0).astype(jnp.bfloat16)
    second_basis = basis_of(hidden, False, degrees)
    theta_cols = lax.dynamic_slice_in_dim(theta_second, out_start, width_out, 2)
    summed = jnp.einsum(
        "kio,kiyx->oyx", theta_cols, second_basis, preferred_element_type=jnp.float32
    )
    bias_cols = lax.dynamic_slice_in_dim(bias_second, out_start, width_out, 0)
    return (summed + bias_cols[:, None, None]).astype(jnp.bfloat16)


def solution(mesh):
    return jax.shard_map(
        per_device,
        mesh=mesh,
        in_specs=(P("shell", "sky", None), P(), P("shell"), P(), P(), P(), P()),
        out_specs=P("shell", "sky", None),
        check_vma=False,
    )
```

profile of v0, /device:TPU:0, one launch (start us, length us, event | category | flops | bytes accessed | tf_op | source)
XLA Modules:
  0.0 148.8 jit_solution(16323545694625500989)
XLA Ops:
  6.5 1.0 fusion.26
  7.5 0.2 copy-done
  7.7 1.0 fusion.24
  8.8 0.7 dynamic_slice.7
  9.5 38.8 %all-reduce.22.cloned.1.call-done = f32[4,48,384]{2,0,1:T(4,128)} async-done(((f32[4,48,384]{2,0,1:T(4,128)}), f32[4,48,384]{2,0,1:T(4,128)}) %all-reduce.22.cloned.1.call-update) | async-done | bytes 294928 | tf_op jit(solution)/shard_map/psum | solution.py:60
  48.3 0.7 fusion.78
  49.0 2.6 %collective-permute-start.1 = (f32[4,1,384]{2,0,1:T(4,128)S(1)}, f32[4,1,384]{2,0,1:T(4,128)S(1)}, u32[]{:S(2)}, u32[]{:S(2)}) collective-permute-start(f32[4,1,384]{2,0,1:T(4,128)S(1)} %get-tuple-element.58), channel_id=1, source_target_pairs={{1,0},{2,1},{3,2},{4,3},{5,4},{6,5},{7,6},{0,7},{9,8},{10,9},{11,1... | collective-permute-start | bytes 18440 | tf_op jit(solution)/shard_map/ppermute | solution.py:16
  51.7 1.3 fusion.79
  52.9 1.0 bitcast_dynamic-update-slice_fusion.11
  54.0 1.3 bitcast_dynamic-update-slice_fusion.10
  55.4 2.6 %collective-permute-start.3 = (f32[4,1,384]{2,0,1:T(4,128)S(1)}, f32[4,1,384]{2,0,1:T(4,128)S(1)}, u32[]{:S(2)}, u32[]{:S(2)}) collective-permute-start(f32[4,1,384]{2,0,1:T(4,128)S(1)} %get-tuple-element.54), channel_id=1, source_target_pairs={{1,0},{2,1},{3,2},{4,3},{5,4},{6,5},{7,6},{0,7},{9,8},{10,9},{11,1... | collective-permute-start | bytes 18440 | tf_op jit(solution)/shard_map/ppermute | solution.py:16
  58.2 1.1 collective-permute-done.2
  59.4 1.3 bitcast_dynamic-update-slice_fusion.9
  60.8 2.6 %collective-permute-start.5 = (f32[4,1,384]{2,0,1:T(4,128)S(1)}, f32[4,1,384]{2,0,1:T(4,128)S(1)}, u32[]{:S(2)}, u32[]{:S(2)}) collective-permute-start(f32[4,1,384]{2,0,1:T(4,128)S(1)} %get-tuple-element.50), channel_id=1, source_target_pairs={{1,0},{2,1},{3,2},{4,3},{5,4},{6,5},{7,6},{0,7},{9,8},{10,9},{11,1... | collective-permute-start | bytes 18440 | tf_op jit(solution)/shard_map/ppermute | solution.py:16
  63.6 1.1 collective-permute-done.4
  64.7 0.3 bitcast_dynamic-update-slice_fusion.8
  65.0 0.5 collective-permute-start.6
  65.5 2.2 %collective-permute-start.7 = (f32[4,1,384]{2,0,1:T(4,128)S(1)}, f32[4,1,384]{2,0,1:T(4,128)S(1)}, u32[]{:S(2)}, u32[]{:S(2)}) collective-permute-start(f32[4,1,384]{2,0,1:T(4,128)S(1)} %get-tuple-element.46), channel_id=1, source_target_pairs={{1,0},{2,1},{3,2},{4,3},{5,4},{6,5},{7,6},{0,7},{9,8},{10,9},{11,1... | collective-permute-start | bytes 18440 | tf_op jit(solution)/shard_map/ppermute | solution.py:16
  67.9 1.1 collective-permute-done.6
  69.1 0.3 bitcast_dynamic-update-slice_fusion.7
  69.4 0.5 collective-permute-start.8
  69.8 2.2 %collective-permute-start.9 = (f32[4,1,384]{2,0,1:T(4,128)S(1)}, f32[4,1,384]{2,0,1:T(4,128)S(1)}, u32[]{:S(2)}, u32[]{:S(2)}) collective-permute-start(f32[4,1,384]{2,0,1:T(4,128)S(1)} %get-tuple-element.42), channel_id=1, source_target_pairs={{1,0},{2,1},{3,2},{4,3},{5,4},{6,5},{7,6},{0,7},{9,8},{10,9},{11,1... | collective-permute-start | bytes 18440 | tf_op jit(solution)/shard_map/ppermute | solution.py:16
  72.3 1.1 collective-permute-done.8
  73.4 0.3 bitcast_dynamic-update-slice_fusion.6
  73.7 2.5 %bitcast_dynamic-update-slice_fusion = (bf16[6,64,48,384]{3,1,2,0:T(8,128)(2,1)}, bf16[48,384,64]{1,2,0:T(8,128)(2,1)S(1)}) fusion(f32[64]{0:T(128)S(1)} %copy-done.5, bf16[6,4,48,384]{3,1,2,0:T(4,128)(2,1)S(1)} %bitcast_dynamic-update-slice_fusion.6, bf16[6,4,64]{2,1,0:T(4,128)(2,1)S(1)} %copy-done.4), kind=kOutput, calls=%fused_computation.33 | convolution fusion | flops 60162048 | bytes 5606656 | tf_op jit(solution)/shard_map/kbo,kbyx->oyx/dot_general | solution.py:66
  76.2 0.6 bitcast_convert_fusion
  76.8 0.5 collective-permute-start.10
  77.3 0.3 copy-done.2
  77.6 2.6 %collective-permute-start.11 = (f32[64,1,384]{2,0,1:T(8,128)S(1)}, f32[64,1,384]{2,0,1:T(8,128)S(1)}, u32[]{:S(2)}, u32[]{:S(2)}) collective-permute-start(f32[64,1,384]{2,0,1:T(8,128)S(1)} %get-tuple-element.38), channel_id=1, source_target_pairs={{1,0},{2,1},{3,2},{4,3},{5,4},{6,5},{7,6},{0,7},{9,8},{10,9},{11,1... | collective-permute-start | bytes 294920 | tf_op jit(solution)/shard_map/ppermute | solution.py:16
  80.2 1.8 %fusion.69 = (f32[64,48,383]{2,0,1:T(8,128)S(1)}, f32[64,48,383]{2,0,1:T(8,128)S(1)}) fusion(f32[64,48,384]{2,0,1:T(8,128)S(1)} %bitcast_convert_fusion), kind=kLoop, calls=%fused_computation.98 | loop fusion | bytes 18825216 | tf_op jit(solution)/shard_map/slice | solution.py:22
  82.4 3.7 %bitcast_dynamic-update-slice_fusion.5 = (bf16[6,64,48,384]{3,1,2,0:T(8,128)(2,1)}, f32[64,48,384]{2,0,1:T(8,128)S(1)}) fusion(bf16[6,64,48,384]{3,1,2,0:T(8,128)(2,1)} %get-tuple-element.61, f32[64,48,383]{2,0,1:T(8,128)S(1)} %get-tuple-element.40, f32[64,48,383]{2,0,1:T(8,128)S(1)} %get-tuple-element.39, f32[64,1,384]{2,0,1:T(8,128)S(1)} %collective-permute-done.11, ...), kind=kLoop, calls=%fused_computation.38 | loop fusion | flops 8257536 | bytes 21405696
  86.1 0.4 collective-permute-start.12
  86.5 2.5 %collective-permute-start.13 = (f32[64,1,384]{2,0,1:T(8,128)S(1)}, f32[64,1,384]{2,0,1:T(8,128)S(1)}, u32[]{:S(2)}, u32[]{:S(2)}) collective-permute-start(f32[64,1,384]{2,0,1:T(8,128)S(1)} %get-tuple-element.34), channel_id=1, source_target_pairs={{1,0},{2,1},{3,2},{4,3},{5,4},{6,5},{7,6},{0,7},{9,8},{10,9},{11,1... | collective-permute-start | bytes 294920 | tf_op jit(solution)/shard_map/ppermute | solution.py:16
  89.0 1.8 %fusion.67 = (f32[64,48,383]{2,0,1:T(8,128)S(1)}, f32[64,48,383]{2,0,1:T(8,128)S(1)}) fusion(f32[64,48,384]{2,0,1:T(8,128)S(1)} %get-tuple-element.12), kind=kLoop, calls=%fused_computation.96 | loop fusion | bytes 18825216 | tf_op jit(solution)/shard_map/slice | solution.py:22
  90.8 0.8 collective-permute-done.12
  91.6 5.3 %bitcast_dynamic-update-slice_fusion.4 = (bf16[6,64,48,384]{3,1,2,0:T(8,128)(2,1)}, f32[64,48,384]{2,0,1:T(8,128)S(1)}) fusion(bf16[6,64,48,384]{3,1,2,0:T(8,128)(2,1)} %get-tuple-element.11, bf16[48,384,64]{1,2,0:T(8,128)(2,1)} %copy-done.2, f32[64,48,383]{2,0,1:T(8,128)S(1)} %get-tuple-element.36, f32[64,48,383]{2,0,1:T(8,128)S(1)} %get-tuple-element.35, ...), kind=kLoop, calls=%fused_computation.37 | loop fusion | flops 10616832 | bytes 23764992
  96.9 0.5 collective-permute-start.14
  97.4 2.2 %collective-permute-start.15 = (f32[64,1,384]{2,0,1:T(8,128)S(1)}, f32[64,1,384]{2,0,1:T(8,128)S(1)}, u32[]{:S(2)}, u32[]{:S(2)}) collective-permute-start(f32[64,1,384]{2,0,1:T(8,128)S(1)} %get-tuple-element.30), channel_id=1, source_target_pairs={{1,0},{2,1},{3,2},{4,3},{5,4},{6,5},{7,6},{0,7},{9,8},{10,9},{11,1... | collective-permute-start | bytes 294920 | tf_op jit(solution)/shard_map/ppermute | solution.py:16
  99.6 3.8 %fusion.65 = (f32[64,48,383]{2,0,1:T(8,128)S(1)}, f32[64,48,383]{2,0,1:T(8,128)}) fusion(f32[64,48,384]{2,0,1:T(8,128)S(1)} %get-tuple-element.10), kind=kLoop, calls=%fused_computation.94 | loop fusion | bytes 18825216 | tf_op jit(solution)/shard_map/slice | solution.py:22
  103.4 5.9 %bitcast_dynamic-update-slice_fusion.3 = (bf16[6,64,48,384]{3,1,2,0:T(8,128)(2,1)}, f32[64,48,384]{2,0,1:T(8,128)S(1)}) fusion(bf16[6,64,48,384]{3,1,2,0:T(8,128)(2,1)} %get-tuple-element.9, f32[64,48,384]{2,0,1:T(8,128)S(1)} %get-tuple-element.12, f32[64,48,383]{2,0,1:T(8,128)} %get-tuple-element.32, f32[64,48,383]{2,0,1:T(8,128)S(1)} %get-tuple-element.31, ...), kind=kLoop, calls=%fused_computation.36 | loop fusion | flops 9437184 | bytes 26136576
  109.4 2.6 %collective-permute-start.17 = (f32[64,1,384]{2,0,1:T(8,128)S(1)}, f32[64,1,384]{2,0,1:T(8,128)S(1)}, u32[]{:S(2)}, u32[]{:S(2)}) collective-permute-start(f32[64,1,384]{2,0,1:T(8,128)S(1)} %get-tuple-element.26), channel_id=1, source_target_pairs={{1,0},{2,1},{3,2},{4,3},{5,4},{6,5},{7,6},{0,7},{9,8},{10,9},{11,1... | collective-permute-start | bytes 294920 | tf_op jit(solution)/shard_map/ppermute | solution.py:16
  112.1 3.8 %fusion.63 = (f32[64,48,383]{2,0,1:T(8,128)S(1)}, f32[64,48,383]{2,0,1:T(8,128)}) fusion(f32[64,48,384]{2,0,1:T(8,128)S(1)} %get-tuple-element.8), kind=kLoop, calls=%fused_computation.92 | loop fusion | bytes 18825216 | tf_op jit(solution)/shard_map/slice | solution.py:22
  115.9 5.8 %bitcast_dynamic-update-slice_fusion.2 = (bf16[6,64,48,384]{3,1,2,0:T(8,128)(2,1)}, f32[64,48,384]{2,0,1:T(8,128)S(1)}) fusion(bf16[6,64,48,384]{3,1,2,0:T(8,128)(2,1)} %get-tuple-element.7, f32[64,48,384]{2,0,1:T(8,128)S(1)} %get-tuple-element.10, f32[64,48,383]{2,0,1:T(8,128)} %get-tuple-element.28, f32[64,48,383]{2,0,1:T(8,128)S(1)} %get-tuple-element.27, ...), kind=kLoop, calls=%fused_computation.35 | loop fusion | flops 9437184 | bytes 26136576
  121.8 2.6 %collective-permute-start.19 = (f32[64,1,384]{2,0,1:T(8,128)S(1)}, f32[64,1,384]{2,0,1:T(8,128)S(1)}, u32[]{:S(2)}, u32[]{:S(2)}) collective-permute-start(f32[64,1,384]{2,0,1:T(8,128)S(1)} %get-tuple-element.22), channel_id=1, source_target_pairs={{1,0},{2,1},{3,2},{4,3},{5,4},{6,5},{7,6},{0,7},{9,8},{10,9},{11,1... | collective-permute-start | bytes 294920 | tf_op jit(solution)/shard_map/ppermute | solution.py:16
  124.4 3.8 %fusion.61 = (f32[64,48,383]{2,0,1:T(8,128)S(1)}, f32[64,48,383]{2,0,1:T(8,128)}) fusion(f32[64,48,384]{2,0,1:T(8,128)S(1)} %get-tuple-element.6), kind=kLoop, calls=%fused_computation.90 | loop fusion | bytes 18825216 | tf_op jit(solution)/shard_map/slice | solution.py:22
  128.2 5.7 %bitcast_dynamic-update-slice_fusion.1 = bf16[6,64,48,384]{3,1,2,0:T(8,128)(2,1)} fusion(bf16[6,64,48,384]{3,1,2,0:T(8,128)(2,1)} %get-tuple-element.5, f32[64,48,384]{2,0,1:T(8,128)S(1)} %get-tuple-element.8, f32[64,48,383]{2,0,1:T(8,128)} %get-tuple-element.24, f32[64,48,383]{2,0,1:T(8,128)S(1)} %get-tuple-element.23, ...), kind=kLoop, calls=%fused_computation.34 | loop fusion | flops 9437184 | bytes 21417984 | tf_op jit(solution)/shard_map/stack | solution.py:48
  133.9 7.1 %fusion.23 = bf16[16,48,384]{2,0,1:T(8,128)(2,1)S(1)} fusion(bf16[6,64,48,384]{3,1,2,0:T(8,128)(2,1)} %bitcast_dynamic-update-slice_fusion.1, f32[16]{0:T(128)S(1)} %dynamic_slice.7, bf16[6,64,64]{2,1,0:T(8,128)(2,1)S(1)} %copy-done.3, s32[]{:T(128)S(6)} %select_n.4), kind=kOutput, calls=%fused_computation.42 | convolution fusion | flops 227082240 | bytes 14794820 | tf_op jit(solution)/shard_map/kio,kiyx->oyx/dot_general | solution.py:72
  141.0 0.9 copy.13
  (45 shorter events, 1.9 us)
Async XLA Ops:
  6.5 1.2 copy-start
  6.5 41.8 %all-reduce.22.cloned.1.call-start = ((), (), s32[]{:S(2)}) async-start(), calls=%async_computation | async-start | bytes 589824 | tf_op jit(solution)/shard_map/psum | solution.py:60
  49.0 4.9 %collective-permute-start = (f32[4,1,384]{2,0,1:T(4,128)S(1)}, f32[4,1,384]{2,0,1:T(4,128)S(1)}, u32[]{:S(2)}, u32[]{:S(2)}) collective-permute-start(f32[4,1,384]{2,0,1:T(4,128)S(1)} %get-tuple-element.57), channel_id=1, source_target_pairs={{0,1},{1,2},{2,3},{3,4},{4,5},{5,6},{6,7},{7,0},{8,9},{9,10},{10,1... | collective-permute-start | bytes 18440 | tf_op jit(solution)/shard_map/ppermute | solution.py:13
  49.0 4.9 %collective-permute-start.1 = (f32[4,1,384]{2,0,1:T(4,128)S(1)}, f32[4,1,384]{2,0,1:T(4,128)S(1)}, u32[]{:S(2)}, u32[]{:S(2)}) collective-permute-start(f32[4,1,384]{2,0,1:T(4,128)S(1)} %get-tuple-element.58), channel_id=1, source_target_pairs={{1,0},{2,1},{3,2},{4,3},{5,4},{6,5},{7,6},{0,7},{9,8},{10,9},{11,1... | collective-permute-start | bytes 18440 | tf_op jit(solution)/shard_map/ppermute | solution.py:16
  55.3 4.0 %collective-permute-start.2 = (f32[4,1,384]{2,0,1:T(4,128)S(1)}, f32[4,1,384]{2,0,1:T(4,128)S(1)}, u32[]{:S(2)}, u32[]{:S(2)}) collective-permute-start(f32[4,1,384]{2,0,1:T(4,128)S(1)} %get-tuple-element.53), channel_id=1, source_target_pairs={{0,1},{1,2},{2,3},{3,4},{4,5},{5,6},{6,7},{7,0},{8,9},{9,10},{10,1... | collective-permute-start | bytes 18440 | tf_op jit(solution)/shard_map/ppermute | solution.py:13
  55.4 4.0 %collective-permute-start.3 = (f32[4,1,384]{2,0,1:T(4,128)S(1)}, f32[4,1,384]{2,0,1:T(4,128)S(1)}, u32[]{:S(2)}, u32[]{:S(2)}) collective-permute-start(f32[4,1,384]{2,0,1:T(4,128)S(1)} %get-tuple-element.54), channel_id=1, source_target_pairs={{1,0},{2,1},{3,2},{4,3},{5,4},{6,5},{7,6},{0,7},{9,8},{10,9},{11,1... | collective-permute-start | bytes 18440 | tf_op jit(solution)/shard_map/ppermute | solution.py:16
  59.4 14.3 %copy-start.4 = (bf16[6,4,64]{2,1,0:T(4,128)(2,1)S(1)}, bf16[6,4,64]{2,1,0:T(4,128)(2,1)}, u32[]{:S(2)}) copy-start(bf16[6,4,64]{2,1,0:T(4,128)(2,1)} %param.10) | copy-start | bytes 9220
  59.4 14.3 %copy-start.5 = (f32[64]{0:T(128)S(1)}, f32[64]{0:T(128)}, u32[]{:S(2)}) copy-start(f32[64]{0:T(128)} %param.11) | copy-start | bytes 772
  60.6 4.0 %collective-permute-start.4 = (f32[4,1,384]{2,0,1:T(4,128)S(1)}, f32[4,1,384]{2,0,1:T(4,128)S(1)}, u32[]{:S(2)}, u32[]{:S(2)}) collective-permute-start(f32[4,1,384]{2,0,1:T(4,128)S(1)} %get-tuple-element.49), channel_id=1, source_target_pairs={{0,1},{1,2},{2,3},{3,4},{4,5},{5,6},{6,7},{7,0},{8,9},{9,10},{10,1... | collective-permute-start | bytes 18440 | tf_op jit(solution)/shard_map/ppermute | solution.py:13
  60.8 4.0 %collective-permute-start.5 = (f32[4,1,384]{2,0,1:T(4,128)S(1)}, f32[4,1,384]{2,0,1:T(4,128)S(1)}, u32[]{:S(2)}, u32[]{:S(2)}) collective-permute-start(f32[4,1,384]{2,0,1:T(4,128)S(1)} %get-tuple-element.50), channel_id=1, source_target_pairs={{1,0},{2,1},{3,2},{4,3},{5,4},{6,5},{7,6},{0,7},{9,8},{10,9},{11,1... | collective-permute-start | bytes 18440 | tf_op jit(solution)/shard_map/ppermute | solution.py:16
  65.0 4.0 %collective-permute-start.6 = (f32[4,1,384]{2,0,1:T(4,128)S(1)}, f32[4,1,384]{2,0,1:T(4,128)S(1)}, u32[]{:S(2)}, u32[]{:S(2)}) collective-permute-start(f32[4,1,384]{2,0,1:T(4,128)S(1)} %get-tuple-element.45), channel_id=1, source_target_pairs={{0,1},{1,2},{2,3},{3,4},{4,5},{5,6},{6,7},{7,0},{8,9},{9,10},{10,1... | collective-permute-start | bytes 18440 | tf_op jit(solution)/shard_map/ppermute | solution.py:13
  65.5 3.6 %collective-permute-start.7 = (f32[4,1,384]{2,0,1:T(4,128)S(1)}, f32[4,1,384]{2,0,1:T(4,128)S(1)}, u32[]{:S(2)}, u32[]{:S(2)}) collective-permute-start(f32[4,1,384]{2,0,1:T(4,128)S(1)} %get-tuple-element.46), channel_id=1, source_target_pairs={{1,0},{2,1},{3,2},{4,3},{5,4},{6,5},{7,6},{0,7},{9,8},{10,9},{11,1... | collective-permute-start | bytes 18440 | tf_op jit(solution)/shard_map/ppermute | solution.py:16
  69.4 4.0 %collective-permute-start.8 = (f32[4,1,384]{2,0,1:T(4,128)S(1)}, f32[4,1,384]{2,0,1:T(4,128)S(1)}, u32[]{:S(2)}, u32[]{:S(2)}) collective-permute-start(f32[4,1,384]{2,0,1:T(4,128)S(1)} %get-tuple-element.41), channel_id=1, source_target_pairs={{0,1},{1,2},{2,3},{3,4},{4,5},{5,6},{6,7},{7,0},{8,9},{9,10},{10,1... | collective-permute-start | bytes 18440 | tf_op jit(solution)/shard_map/ppermute | solution.py:13
  69.8 3.6 %collective-permute-start.9 = (f32[4,1,384]{2,0,1:T(4,128)S(1)}, f32[4,1,384]{2,0,1:T(4,128)S(1)}, u32[]{:S(2)}, u32[]{:S(2)}) collective-permute-start(f32[4,1,384]{2,0,1:T(4,128)S(1)} %get-tuple-element.42), channel_id=1, source_target_pairs={{1,0},{2,1},{3,2},{4,3},{5,4},{6,5},{7,6},{0,7},{9,8},{10,9},{11,1... | collective-permute-start | bytes 18440 | tf_op jit(solution)/shard_map/ppermute | solution.py:16
  76.2 1.4 copy-start.2
  76.8 5.4 %collective-permute-start.10 = (f32[64,1,384]{2,0,1:T(8,128)S(1)}, f32[64,1,384]{2,0,1:T(8,128)S(1)}, u32[]{:S(2)}, u32[]{:S(2)}) collective-permute-start(f32[64,1,384]{2,0,1:T(8,128)S(1)} %get-tuple-element.37), channel_id=1, source_target_pairs={{0,1},{1,2},{2,3},{3,4},{4,5},{5,6},{6,7},{7,0},{8,9},{9,10},{10,1... | collective-permute-start | bytes 294920 | tf_op jit(solution)/shard_map/ppermute | solution.py:13
  77.6 4.8 %collective-permute-start.11 = (f32[64,1,384]{2,0,1:T(8,128)S(1)}, f32[64,1,384]{2,0,1:T(8,128)S(1)}, u32[]{:S(2)}, u32[]{:S(2)}) collective-permute-start(f32[64,1,384]{2,0,1:T(8,128)S(1)} %get-tuple-element.38), channel_id=1, source_target_pairs={{1,0},{2,1},{3,2},{4,3},{5,4},{6,5},{7,6},{0,7},{9,8},{10,9},{11,1... | collective-permute-start | bytes 294920 | tf_op jit(solution)/shard_map/ppermute | solution.py:16
  86.1 5.5 %collective-permute-start.12 = (f32[64,1,384]{2,0,1:T(8,128)S(1)}, f32[64,1,384]{2,0,1:T(8,128)S(1)}, u32[]{:S(2)}, u32[]{:S(2)}) collective-permute-start(f32[64,1,384]{2,0,1:T(8,128)S(1)} %get-tuple-element.33), channel_id=1, source_target_pairs={{0,1},{1,2},{2,3},{3,4},{4,5},{5,6},{6,7},{7,0},{8,9},{9,10},{10,1... | collective-permute-start | bytes 294920 | tf_op jit(solution)/shard_map/ppermute | solution.py:13
  86.5 5.1 %collective-permute-start.13 = (f32[64,1,384]{2,0,1:T(8,128)S(1)}, f32[64,1,384]{2,0,1:T(8,128)S(1)}, u32[]{:S(2)}, u32[]{:S(2)}) collective-permute-start(f32[64,1,384]{2,0,1:T(8,128)S(1)} %get-tuple-element.34), channel_id=1, source_target_pairs={{1,0},{2,1},{3,2},{4,3},{5,4},{6,5},{7,6},{0,7},{9,8},{10,9},{11,1... | collective-permute-start | bytes 294920 | tf_op jit(solution)/shard_map/ppermute | solution.py:16
  96.9 6.5 %collective-permute-start.14 = (f32[64,1,384]{2,0,1:T(8,128)S(1)}, f32[64,1,384]{2,0,1:T(8,128)S(1)}, u32[]{:S(2)}, u32[]{:S(2)}) collective-permute-start(f32[64,1,384]{2,0,1:T(8,128)S(1)} %get-tuple-element.29), channel_id=1, source_target_pairs={{0,1},{1,2},{2,3},{3,4},{4,5},{5,6},{6,7},{7,0},{8,9},{9,10},{10,1... | collective-permute-start | bytes 294920 | tf_op jit(solution)/shard_map/ppermute | solution.py:13
  97.4 6.0 %collective-permute-start.15 = (f32[64,1,384]{2,0,1:T(8,128)S(1)}, f32[64,1,384]{2,0,1:T(8,128)S(1)}, u32[]{:S(2)}, u32[]{:S(2)}) collective-permute-start(f32[64,1,384]{2,0,1:T(8,128)S(1)} %get-tuple-element.30), channel_id=1, source_target_pairs={{1,0},{2,1},{3,2},{4,3},{5,4},{6,5},{7,6},{0,7},{9,8},{10,9},{11,1... | collective-permute-start | bytes 294920 | tf_op jit(solution)/shard_map/ppermute | solution.py:16
  109.4 6.5 %collective-permute-start.16 = (f32[64,1,384]{2,0,1:T(8,128)S(1)}, f32[64,1,384]{2,0,1:T(8,128)S(1)}, u32[]{:S(2)}, u32[]{:S(2)}) collective-permute-start(f32[64,1,384]{2,0,1:T(8,128)S(1)} %get-tuple-element.25), channel_id=1, source_target_pairs={{0,1},{1,2},{2,3},{3,4},{4,5},{5,6},{6,7},{7,0},{8,9},{9,10},{10,1... | collective-permute-start | bytes 294920 | tf_op jit(solution)/shard_map/ppermute | solution.py:13
  109.4 6.4 %collective-permute-start.17 = (f32[64,1,384]{2,0,1:T(8,128)S(1)}, f32[64,1,384]{2,0,1:T(8,128)S(1)}, u32[]{:S(2)}, u32[]{:S(2)}) collective-permute-start(f32[64,1,384]{2,0,1:T(8,128)S(1)} %get-tuple-element.26), channel_id=1, source_target_pairs={{1,0},{2,1},{3,2},{4,3},{5,4},{6,5},{7,6},{0,7},{9,8},{10,9},{11,1... | collective-permute-start | bytes 294920 | tf_op jit(solution)/shard_map/ppermute | solution.py:16
  121.7 6.5 %collective-permute-start.18 = (f32[64,1,384]{2,0,1:T(8,128)S(1)}, f32[64,1,384]{2,0,1:T(8,128)S(1)}, u32[]{:S(2)}, u32[]{:S(2)}) collective-permute-start(f32[64,1,384]{2,0,1:T(8,128)S(1)} %get-tuple-element.21), channel_id=1, source_target_pairs={{0,1},{1,2},{2,3},{3,4},{4,5},{5,6},{6,7},{7,0},{8,9},{9,10},{10,1... | collective-permute-start | bytes 294920 | tf_op jit(solution)/shard_map/ppermute | solution.py:13
  121.8 6.4 %collective-permute-start.19 = (f32[64,1,384]{2,0,1:T(8,128)S(1)}, f32[64,1,384]{2,0,1:T(8,128)S(1)}, u32[]{:S(2)}, u32[]{:S(2)}) collective-permute-start(f32[64,1,384]{2,0,1:T(8,128)S(1)} %get-tuple-element.22), channel_id=1, source_target_pairs={{1,0},{2,1},{3,2},{4,3},{5,4},{6,5},{7,6},{0,7},{9,8},{10,9},{11,1... | collective-permute-start | bytes 294920 | tf_op jit(solution)/shard_map/ppermute | solution.py:16
  128.2 5.8 %copy-start.3 = (bf16[6,64,64]{2,1,0:T(8,128)(2,1)S(1)}, bf16[6,64,64]{2,1,0:T(8,128)(2,1)}, u32[]{:S(2)}) copy-start(bf16[6,64,64]{2,1,0:T(8,128)(2,1)} %param.12) | copy-start | bytes 147460
  128.2 13.7 %copy-start.1 = (bf16[25,48,384]{2,1,0:T(8,128)(2,1)S(1)}, bf16[25,48,384]{2,1,0:T(8,128)(2,1)}, u32[]{:S(2)}) copy-start(bf16[25,48,384]{2,1,0:T(8,128)(2,1)} %param.7) | copy-start | bytes 2764804
Sparse Core Ops, SparseCore 0:
  9.7 38.5 all-reduce.21
where the time goes:
time: 149 us
  waiting for transfers between devices  44.6 us (30%)
  other arithmetic  31.4 us (21%)
  starting transfers between devices  27.5 us (18%)
  local copies, waits for them, and re-layouts  20.1 us (13%)
  between operations  13.6 us (9%)
  matrix products  11.5 us (8%)
    psum x1, waiting for transfers between devices, per_device(): convergence = lax.psum(partial_sum, 'shell')  38.8 us
    ppermute x10, starting transfers between devices, padded(): lax.ppermute(lax.slice_in_dim(block, 0, width, axis=dim), axis, backward)  24.9 us
    unnamed x9, other arithmetic  24.8 us
    slice x10, local copies, waits for them, and re-layouts, lateral(): right_side = jnp.pad(source_field[:, :, 1:], ((0, 0), (0, 0), (0, 1)))  17.1 us
    dot_general x1, matrix products, per_device(): jnp.einsum('kio,kiyx->oyx', theta_cols, second_basis, preferred_element_t...  7.06 us
    another operation x2, other arithmetic, basis_of(): return jnp.stack(collected)  5.99 us
    ppermute x10, waiting for transfers between devices, padded(): lax.ppermute(lax.slice_in_dim(block, block.shape[dim] - width, None, axis...  5.37 us
  transfers between devices with their start and end apart: 21, of which 11 were waited for; matrix products, arithmetic and copies ran while one was open for 13% of the time, Pallas kernels for 0%

commit v1 on v0

--- a/solution.py
+++ b/solution.py
@@ -57,7 +57,8 @@
     selector = (shell_row[:, None] == table_ids).astype(jnp.float32)
     weights = jnp.dot(selector, kernel_table, precision=lax.Precision.HIGHEST).astype(jnp.bfloat16)
     partial_sum = jnp.einsum("sb,syx->byx", weights, density, preferred_element_type=jnp.float32)
-    convergence = lax.psum(partial_sum, "shell")
+    z2 = lax.all_gather(partial_sum, axis_name="shell")
+    convergence = jnp.sum(z2, 0)
     first_basis = basis_of(convergence, True, degrees)
     groups = lax.axis_size("shell")
     shell_index = lax.axis_index("shell")

time: 149 us -> 145 us (0.973)
  waiting for transfers between devices: 44.6 us -> 38 us
  local copies, waits for them, and re-layouts: 20.1 us -> 24.7 us
  other arithmetic: 31.4 us -> 29.7 us
    psum x1 -> x0, waiting for transfers between devices: 38.8 us -> none  [per_device(): convergence = lax.psum(partial_sum, 'shell')]
    all_gather x0 -> x1, waiting for transfers between devices: none -> 32.6 us  [per_device(): z2 = lax.all_gather(partial_sum, axis_name='shell')]
    another operation x0 -> x6, local copies, waits for them, and re-layouts: none -> 5.16 us  [basis_of(): return jnp.stack(collected)]
    unnamed x9 -> x4, other arithmetic: 24.8 us -> 20.7 us
    another operation x2 -> x6, other arithmetic: 5.99 us -> 7.01 us  [basis_of(): return jnp.stack(collected)]
  transfers between devices with their start and end apart: 21 -> 21, of which waited for: 11 -> 13; matrix products, arithmetic and copies ran while one was open for 13% -> 12% of each run, Pallas kernels for 0% -> 0%
where the time goes in v1:
time: 145 us
  waiting for transfers between devices  38 us (26%)
  other arithmetic  29.7 us (20%)
  starting transfers between devices  27.8 us (19%)
  local copies, waits for them, and re-layouts  24.7 us (17%)
  between operations  13.7 us (9%)
  matrix products  10.7 us (7%)
    all_gather x1, waiting for transfers between devices, per_device(): z2 = lax.all_gather(partial_sum, axis_name='shell')  32.6 us
    ppermute x10, starting transfers between devices, padded(): lax.ppermute(lax.slice_in_dim(block, 0, width, axis=dim), axis, backward)  24.2 us
    unnamed x4, other arithmetic  20.7 us
    slice x10, local copies, waits for them, and re-layouts, lateral(): right_side = jnp.pad(source_field[:, :, 1:], ((0, 0), (0, 0), (0, 1)))  16.1 us
    dot_general x1, matrix products, per_device(): jnp.einsum('kio,kiyx->oyx', theta_cols, second_basis, preferred_element_t...  7.06 us
    another operation x6, other arithmetic, basis_of(): return jnp.stack(collected)  7.01 us
    another operation x6, local copies, waits for them, and re-layouts, basis_of(): return jnp.stack(collected)  5.16 us
    ppermute x10, waiting for transfers between devices, padded(): lax.ppermute(lax.slice_in_dim(block, block.shape[dim] - width, None, axis...  4.91 us
  transfers between devices with their start and end apart: 21, of which 13 were waited for; matrix products, arithmetic and copies ran while one was open for 12% of the time, Pallas kernels for 0%

profile of v1, /device:TPU:0, one launch (start us, length us, event | category | flops | bytes accessed | tf_op | source)
XLA Modules:
  0.0 144.6 jit_solution(18071467632210101399)
XLA Ops:
  6.5 1.0 fusion.26
  7.7 0.3 fusion.24
  8.0 0.7 copy.96
  8.8 0.7 dynamic_slice.7
  9.5 32.6 %all-gather.3.cloned.1.call-done = f32[16,48,384]{2,1,0:T(8,128)} async-done(((f32[4,48,384]{2,1,0:T(8,128)}), f32[16,48,384]{2,1,0:T(8,128)}) %all-gather.3.cloned.1.call-update) | async-done | bytes 1179664 | tf_op jit(solution)/shard_map/all_gather | solution.py:60
  42.1 1.4 reduce_sum.9
  43.7 2.6 %collective-permute-start.1 = (f32[4,1,384]{2,0,1:T(4,128)S(1)}, f32[4,1,384]{2,0,1:T(4,128)S(1)}, u32[]{:S(2)}, u32[]{:S(2)}) collective-permute-start(f32[4,1,384]{2,0,1:T(4,128)S(1)} %get-tuple-element.58), channel_id=1, source_target_pairs={{1,0},{2,1},{3,2},{4,3},{5,4},{6,5},{7,6},{0,7},{9,8},{10,9},{11,1... | collective-permute-start | bytes 18440 | tf_op jit(solution)/shard_map/ppermute | solution.py:16
  46.9 0.7 collective-permute-done
  47.9 0.7 collective-permute-start.2
  48.6 2.0 %collective-permute-start.3 = (f32[4,1,384]{2,0,1:T(4,128)S(1)}, f32[4,1,384]{2,0,1:T(4,128)S(1)}, u32[]{:S(2)}, u32[]{:S(2)}) collective-permute-start(f32[4,1,384]{2,0,1:T(4,128)S(1)} %get-tuple-element.54), channel_id=1, source_target_pairs={{1,0},{2,1},{3,2},{4,3},{5,4},{6,5},{7,6},{0,7},{9,8},{10,9},{11,1... | collective-permute-start | bytes 18440 | tf_op jit(solution)/shard_map/ppermute | solution.py:16
  51.1 0.8 collective-permute-done.2
  52.0 0.3 convert_bitcast_fusion.2
  52.3 0.5 collective-permute-start.4
  52.8 2.2 %collective-permute-start.5 = (f32[4,1,384]{2,0,1:T(4,128)S(1)}, f32[4,1,384]{2,0,1:T(4,128)S(1)}, u32[]{:S(2)}, u32[]{:S(2)}) collective-permute-start(f32[4,1,384]{2,0,1:T(4,128)S(1)} %get-tuple-element.50), channel_id=1, source_target_pairs={{1,0},{2,1},{3,2},{4,3},{5,4},{6,5},{7,6},{0,7},{9,8},{10,9},{11,1... | collective-permute-start | bytes 18440 | tf_op jit(solution)/shard_map/ppermute | solution.py:16
  55.5 0.8 collective-permute-done.4
  56.4 0.2 convert_bitcast_fusion.1
  56.7 0.5 collective-permute-start.6
  57.1 2.3 %collective-permute-start.7 = (f32[4,1,384]{2,0,1:T(4,128)S(1)}, f32[4,1,384]{2,0,1:T(4,128)S(1)}, u32[]{:S(2)}, u32[]{:S(2)}) collective-permute-start(f32[4,1,384]{2,0,1:T(4,128)S(1)} %get-tuple-element.46), channel_id=1, source_target_pairs={{1,0},{2,1},{3,2},{4,3},{5,4},{6,5},{7,6},{0,7},{9,8},{10,9},{11,1... | collective-permute-start | bytes 18440 | tf_op jit(solution)/shard_map/ppermute | solution.py:16
  59.9 0.8 collective-permute-done.6
  60.7 0.2 convert_bitcast_fusion
  61.0 0.5 collective-permute-start.8
  61.5 2.3 %collective-permute-start.9 = (f32[4,1,384]{2,0,1:T(4,128)S(1)}, f32[4,1,384]{2,0,1:T(4,128)S(1)}, u32[]{:S(2)}, u32[]{:S(2)}) collective-permute-start(f32[4,1,384]{2,0,1:T(4,128)S(1)} %get-tuple-element.42), channel_id=1, source_target_pairs={{1,0},{2,1},{3,2},{4,3},{5,4},{6,5},{7,6},{0,7},{9,8},{10,9},{11,1... | collective-permute-start | bytes 18440 | tf_op jit(solution)/shard_map/ppermute | solution.py:16
  64.2 0.8 collective-permute-done.8
  65.6 4.0 %stack.45 = bf16[6,4,48,384]{3,0,1,2:T(8,128)(2,1)S(1)} concatenate(bf16[1,4,48,384]{3,0,1,2:T(2,128)(2,1)S(1)} %copy.104, bf16[1,4,48,384]{3,0,1,2:T(2,128)(2,1)S(1)} %copy.105, bf16[1,4,48,384]{3,0,1,2:T(2,128)(2,1)S(1)} %copy.106, bf16[1,4,48,384]{3,0,1,2:T(2,128)(2,1)S(1)} %copy.107, bf16[1,4,48,384]{3,0,1,2:T(2,128)(2,1)S(1)} %copy.108, bf16[1,4,48,384]{3,0,1,2:T(2,128)(2,1)S(1)} %copy.109), dimensions={0} | concatenate | bytes 1769472 | tf_op jit(solution)/shard_map/stack | solution.py:48
  69.6 2.4 %bitcast_dynamic-update-slice_fusion = (bf16[6,64,48,384]{3,1,2,0:T(8,128)(2,1)}, bf16[48,384,64]{1,2,0:T(8,128)(2,1)S(1)}) fusion(f32[64]{0:T(128)S(1)} %copy-done.5, bf16[6,4,48,384]{3,0,1,2:T(8,128)(2,1)S(1)} %stack.45, bf16[6,4,64]{2,1,0:T(4,128)(2,1)S(1)} %copy-done.4), kind=kOutput, calls=%fused_computation.33 | convolution fusion | flops 60162048 | bytes 5606656 | tf_op jit(solution)/shard_map/kbo,kbyx->oyx/dot_general | solution.py:67
  72.0 0.6 bitcast_convert_fusion
  72.7 0.5 collective-permute-start.10
  73.1 0.3 copy-done.2
  73.4 2.6 %collective-permute-start.11 = (f32[64,1,384]{2,0,1:T(8,128)S(1)}, f32[64,1,384]{2,0,1:T(8,128)S(1)}, u32[]{:S(2)}, u32[]{:S(2)}) collective-permute-start(f32[64,1,384]{2,0,1:T(8,128)S(1)} %get-tuple-element.38), channel_id=1, source_target_pairs={{1,0},{2,1},{3,2},{4,3},{5,4},{6,5},{7,6},{0,7},{9,8},{10,9},{11,1... | collective-permute-start | bytes 294920 | tf_op jit(solution)/shard_map/ppermute | solution.py:16
  76.0 1.8 %fusion.71 = (f32[64,48,383]{2,0,1:T(8,128)S(1)}, f32[64,48,383]{2,0,1:T(8,128)S(1)}) fusion(f32[64,48,384]{2,0,1:T(8,128)S(1)} %bitcast_convert_fusion), kind=kLoop, calls=%fused_computation.99 | loop fusion | bytes 18825216 | tf_op jit(solution)/shard_map/slice | solution.py:22
  78.2 3.7 %bitcast_dynamic-update-slice_fusion.5 = (bf16[6,64,48,384]{3,1,2,0:T(8,128)(2,1)}, f32[64,48,384]{2,0,1:T(8,128)S(1)}) fusion(bf16[6,64,48,384]{3,1,2,0:T(8,128)(2,1)} %get-tuple-element.61, f32[64,48,383]{2,0,1:T(8,128)S(1)} %get-tuple-element.40, f32[64,48,383]{2,0,1:T(8,128)S(1)} %get-tuple-element.39, f32[64,1,384]{2,0,1:T(8,128)S(1)} %collective-permute-done.11, ...), kind=kLoop, calls=%fused_computation.38 | loop fusion | flops 8257536 | bytes 21405696
  82.0 0.4 collective-permute-start.12
  82.3 2.7 %collective-permute-start.13 = (f32[64,1,384]{2,0,1:T(8,128)S(1)}, f32[64,1,384]{2,0,1:T(8,128)S(1)}, u32[]{:S(2)}, u32[]{:S(2)}) collective-permute-start(f32[64,1,384]{2,0,1:T(8,128)S(1)} %get-tuple-element.34), channel_id=1, source_target_pairs={{1,0},{2,1},{3,2},{4,3},{5,4},{6,5},{7,6},{0,7},{9,8},{10,9},{11,1... | collective-permute-start | bytes 294920 | tf_op jit(solution)/shard_map/ppermute | solution.py:16
  85.0 1.8 %fusion.69 = (f32[64,48,383]{2,0,1:T(8,128)S(1)}, f32[64,48,383]{2,0,1:T(8,128)S(1)}) fusion(f32[64,48,384]{2,0,1:T(8,128)S(1)} %get-tuple-element.12), kind=kLoop, calls=%fused_computation.97 | loop fusion | bytes 18825216 | tf_op jit(solution)/shard_map/slice | solution.py:22
  86.8 0.7 collective-permute-done.12
  87.4 5.3 %bitcast_dynamic-update-slice_fusion.4 = (bf16[6,64,48,384]{3,1,2,0:T(8,128)(2,1)}, f32[64,48,384]{2,0,1:T(8,128)S(1)}) fusion(bf16[6,64,48,384]{3,1,2,0:T(8,128)(2,1)} %get-tuple-element.11, bf16[48,384,64]{1,2,0:T(8,128)(2,1)} %copy-done.2, f32[64,48,383]{2,0,1:T(8,128)S(1)} %get-tuple-element.36, f32[64,48,383]{2,0,1:T(8,128)S(1)} %get-tuple-element.35, ...), kind=kLoop, calls=%fused_computation.37 | loop fusion | flops 10616832 | bytes 23764992
  92.7 0.5 collective-permute-start.14
  93.2 2.2 %collective-permute-start.15 = (f32[64,1,384]{2,0,1:T(8,128)S(1)}, f32[64,1,384]{2,0,1:T(8,128)S(1)}, u32[]{:S(2)}, u32[]{:S(2)}) collective-permute-start(f32[64,1,384]{2,0,1:T(8,128)S(1)} %get-tuple-element.30), channel_id=1, source_target_pairs={{1,0},{2,1},{3,2},{4,3},{5,4},{6,5},{7,6},{0,7},{9,8},{10,9},{11,1... | collective-permute-start | bytes 294920 | tf_op jit(solution)/shard_map/ppermute | solution.py:16
  95.4 3.8 %fusion.67 = (f32[64,48,383]{2,0,1:T(8,128)S(1)}, f32[64,48,383]{2,0,1:T(8,128)}) fusion(f32[64,48,384]{2,0,1:T(8,128)S(1)} %get-tuple-element.10), kind=kLoop, calls=%fused_computation.95 | loop fusion | bytes 18825216 | tf_op jit(solution)/shard_map/slice | solution.py:22
  99.2 5.9 %bitcast_dynamic-update-slice_fusion.3 = (bf16[6,64,48,384]{3,1,2,0:T(8,128)(2,1)}, f32[64,48,384]{2,0,1:T(8,128)S(1)}) fusion(bf16[6,64,48,384]{3,1,2,0:T(8,128)(2,1)} %get-tuple-element.9, f32[64,48,384]{2,0,1:T(8,128)S(1)} %get-tuple-element.12, f32[64,48,383]{2,0,1:T(8,128)} %get-tuple-element.32, f32[64,48,383]{2,0,1:T(8,128)S(1)} %get-tuple-element.31, ...), kind=kLoop, calls=%fused_computation.36 | loop fusion | flops 9437184 | bytes 26136576
  105.2 2.6 %collective-permute-start.17 = (f32[64,1,384]{2,0,1:T(8,128)S(1)}, f32[64,1,384]{2,0,1:T(8,128)S(1)}, u32[]{:S(2)}, u32[]{:S(2)}) collective-permute-start(f32[64,1,384]{2,0,1:T(8,128)S(1)} %get-tuple-element.26), channel_id=1, source_target_pairs={{1,0},{2,1},{3,2},{4,3},{5,4},{6,5},{7,6},{0,7},{9,8},{10,9},{11,1... | collective-permute-start | bytes 294920 | tf_op jit(solution)/shard_map/ppermute | solution.py:16
  107.9 3.8 %fusion.65 = (f32[64,48,383]{2,0,1:T(8,128)S(1)}, f32[64,48,383]{2,0,1:T(8,128)}) fusion(f32[64,48,384]{2,0,1:T(8,128)S(1)} %get-tuple-element.8), kind=kLoop, calls=%fused_computation.93 | loop fusion | bytes 18825216 | tf_op jit(solution)/shard_map/slice | solution.py:22
  111.7 5.8 %bitcast_dynamic-update-slice_fusion.2 = (bf16[6,64,48,384]{3,1,2,0:T(8,128)(2,1)}, f32[64,48,384]{2,0,1:T(8,128)S(1)}) fusion(bf16[6,64,48,384]{3,1,2,0:T(8,128)(2,1)} %get-tuple-element.7, f32[64,48,384]{2,0,1:T(8,128)S(1)} %get-tuple-element.10, f32[64,48,383]{2,0,1:T(8,128)} %get-tuple-element.28, f32[64,48,383]{2,0,1:T(8,128)S(1)} %get-tuple-element.27, ...), kind=kLoop, calls=%fused_computation.35 | loop fusion | flops 9437184 | bytes 26136576
  117.6 2.6 %collective-permute-start.19 = (f32[64,1,384]{2,0,1:T(8,128)S(1)}, f32[64,1,384]{2,0,1:T(8,128)S(1)}, u32[]{:S(2)}, u32[]{:S(2)}) collective-permute-start(f32[64,1,384]{2,0,1:T(8,128)S(1)} %get-tuple-element.22), channel_id=1, source_target_pairs={{1,0},{2,1},{3,2},{4,3},{5,4},{6,5},{7,6},{0,7},{9,8},{10,9},{11,1... | collective-permute-start | bytes 294920 | tf_op jit(solution)/shard_map/ppermute | solution.py:16
  120.2 3.8 %fusion.63 = (f32[64,48,383]{2,0,1:T(8,128)S(1)}, f32[64,48,383]{2,0,1:T(8,128)}) fusion(f32[64,48,384]{2,0,1:T(8,128)S(1)} %get-tuple-element.6), kind=kLoop, calls=%fused_computation.91 | loop fusion | bytes 18825216 | tf_op jit(solution)/shard_map/slice | solution.py:22
  124.0 5.7 %bitcast_dynamic-update-slice_fusion.1 = bf16[6,64,48,384]{3,1,2,0:T(8,128)(2,1)} fusion(bf16[6,64,48,384]{3,1,2,0:T(8,128)(2,1)} %get-tuple-element.5, f32[64,48,384]{2,0,1:T(8,128)S(1)} %get-tuple-element.8, f32[64,48,383]{2,0,1:T(8,128)} %get-tuple-element.24, f32[64,48,383]{2,0,1:T(8,128)S(1)} %get-tuple-element.23, ...), kind=kLoop, calls=%fused_computation.34 | loop fusion | flops 9437184 | bytes 21417984 | tf_op jit(solution)/shard_map/stack | solution.py:48
  129.8 7.1 %fusion.23 = bf16[16,48,384]{2,0,1:T(8,128)(2,1)S(1)} fusion(bf16[6,64,48,384]{3,1,2,0:T(8,128)(2,1)} %bitcast_dynamic-update-slice_fusion.1, f32[16]{0:T(128)S(1)} %dynamic_slice.7, bf16[6,64,64]{2,1,0:T(8,128)(2,1)S(1)} %copy-done.3, s32[]{:T(128)S(6)} %select_n.4), kind=kOutput, calls=%fused_computation.42 | convolution fusion | flops 227082240 | bytes 14794820 | tf_op jit(solution)/shard_map/kio,kiyx->oyx/dot_general | solution.py:73
  136.8 0.9 copy.112
  (55 shorter events, 4.4 us)
Async XLA Ops:
  6.5 1.2 copy-start
  6.5 35.6 %all-gather.3.cloned.1.call-start = ((), (), s32[]{:S(2)}) async-start(), calls=%async_computation | async-start | bytes 1474560 | tf_op jit(solution)/shard_map/all_gather | solution.py:60
  43.6 4.0 %collective-permute-start = (f32[4,1,384]{2,0,1:T(4,128)S(1)}, f32[4,1,384]{2,0,1:T(4,128)S(1)}, u32[]{:S(2)}, u32[]{:S(2)}) collective-permute-start(f32[4,1,384]{2,0,1:T(4,128)S(1)} %get-tuple-element.57), channel_id=1, source_target_pairs={{0,1},{1,2},{2,3},{3,4},{4,5},{5,6},{6,7},{7,0},{8,9},{9,10},{10,1... | collective-permute-start | bytes 18440 | tf_op jit(solution)/shard_map/ppermute | solution.py:13
  43.7 4.0 %collective-permute-start.1 = (f32[4,1,384]{2,0,1:T(4,128)S(1)}, f32[4,1,384]{2,0,1:T(4,128)S(1)}, u32[]{:S(2)}, u32[]{:S(2)}) collective-permute-start(f32[4,1,384]{2,0,1:T(4,128)S(1)} %get-tuple-element.58), channel_id=1, source_target_pairs={{1,0},{2,1},{3,2},{4,3},{5,4},{6,5},{7,6},{0,7},{9,8},{10,9},{11,1... | collective-permute-start | bytes 18440 | tf_op jit(solution)/shard_map/ppermute | solution.py:16
  47.9 4.0 %collective-permute-start.2 = (f32[4,1,384]{2,0,1:T(4,128)S(1)}, f32[4,1,384]{2,0,1:T(4,128)S(1)}, u32[]{:S(2)}, u32[]{:S(2)}) collective-permute-start(f32[4,1,384]{2,0,1:T(4,128)S(1)} %get-tuple-element.53), channel_id=1, source_target_pairs={{0,1},{1,2},{2,3},{3,4},{4,5},{5,6},{6,7},{7,0},{8,9},{9,10},{10,1... | collective-permute-start | bytes 18440 | tf_op jit(solution)/shard_map/ppermute | solution.py:13
  48.6 3.4 %collective-permute-start.3 = (f32[4,1,384]{2,0,1:T(4,128)S(1)}, f32[4,1,384]{2,0,1:T(4,128)S(1)}, u32[]{:S(2)}, u32[]{:S(2)}) collective-permute-start(f32[4,1,384]{2,0,1:T(4,128)S(1)} %get-tuple-element.54), channel_id=1, source_target_pairs={{1,0},{2,1},{3,2},{4,3},{5,4},{6,5},{7,6},{0,7},{9,8},{10,9},{11,1... | collective-permute-start | bytes 18440 | tf_op jit(solution)/shard_map/ppermute | solution.py:16
  52.3 4.0 %collective-permute-start.4 = (f32[4,1,384]{2,0,1:T(4,128)S(1)}, f32[4,1,384]{2,0,1:T(4,128)S(1)}, u32[]{:S(2)}, u32[]{:S(2)}) collective-permute-start(f32[4,1,384]{2,0,1:T(4,128)S(1)} %get-tuple-element.49), channel_id=1, source_target_pairs={{0,1},{1,2},{2,3},{3,4},{4,5},{5,6},{6,7},{7,0},{8,9},{9,10},{10,1... | collective-permute-start | bytes 18440 | tf_op jit(solution)/shard_map/ppermute | solution.py:13
  52.8 3.6 %collective-permute-start.5 = (f32[4,1,384]{2,0,1:T(4,128)S(1)}, f32[4,1,384]{2,0,1:T(4,128)S(1)}, u32[]{:S(2)}, u32[]{:S(2)}) collective-permute-start(f32[4,1,384]{2,0,1:T(4,128)S(1)} %get-tuple-element.50), channel_id=1, source_target_pairs={{1,0},{2,1},{3,2},{4,3},{5,4},{6,5},{7,6},{0,7},{9,8},{10,9},{11,1... | collective-permute-start | bytes 18440 | tf_op jit(solution)/shard_map/ppermute | solution.py:16
  56.7 4.0 %collective-permute-start.6 = (f32[4,1,384]{2,0,1:T(4,128)S(1)}, f32[4,1,384]{2,0,1:T(4,128)S(1)}, u32[]{:S(2)}, u32[]{:S(2)}) collective-permute-start(f32[4,1,384]{2,0,1:T(4,128)S(1)} %get-tuple-element.45), channel_id=1, source_target_pairs={{0,1},{1,2},{2,3},{3,4},{4,5},{5,6},{6,7},{7,0},{8,9},{9,10},{10,1... | collective-permute-start | bytes 18440 | tf_op jit(solution)/shard_map/ppermute | solution.py:13
  57.1 12.5 %copy-start.4 = (bf16[6,4,64]{2,1,0:T(4,128)(2,1)S(1)}, bf16[6,4,64]{2,1,0:T(4,128)(2,1)}, u32[]{:S(2)}) copy-start(bf16[6,4,64]{2,1,0:T(4,128)(2,1)} %param.10) | copy-start | bytes 9220
  57.1 12.5 %copy-start.5 = (f32[64]{0:T(128)S(1)}, f32[64]{0:T(128)}, u32[]{:S(2)}) copy-start(f32[64]{0:T(128)} %param.11) | copy-start | bytes 772
  57.1 3.6 %collective-permute-start.7 = (f32[4,1,384]{2,0,1:T(4,128)S(1)}, f32[4,1,384]{2,0,1:T(4,128)S(1)}, u32[]{:S(2)}, u32[]{:S(2)}) collective-permute-start(f32[4,1,384]{2,0,1:T(4,128)S(1)} %get-tuple-element.46), channel_id=1, source_target_pairs={{1,0},{2,1},{3,2},{4,3},{5,4},{6,5},{7,6},{0,7},{9,8},{10,9},{11,1... | collective-permute-start | bytes 18440 | tf_op jit(solution)/shard_map/ppermute | solution.py:16
  61.0 4.0 %collective-permute-start.8 = (f32[4,1,384]{2,0,1:T(4,128)S(1)}, f32[4,1,384]{2,0,1:T(4,128)S(1)}, u32[]{:S(2)}, u32[]{:S(2)}) collective-permute-start(f32[4,1,384]{2,0,1:T(4,128)S(1)} %get-tuple-element.41), channel_id=1, source_target_pairs={{0,1},{1,2},{2,3},{3,4},{4,5},{5,6},{6,7},{7,0},{8,9},{9,10},{10,1... | collective-permute-start | bytes 18440 | tf_op jit(solution)/shard_map/ppermute | solution.py:13
  61.5 3.6 %collective-permute-start.9 = (f32[4,1,384]{2,0,1:T(4,128)S(1)}, f32[4,1,384]{2,0,1:T(4,128)S(1)}, u32[]{:S(2)}, u32[]{:S(2)}) collective-permute-start(f32[4,1,384]{2,0,1:T(4,128)S(1)} %get-tuple-element.42), channel_id=1, source_target_pairs={{1,0},{2,1},{3,2},{4,3},{5,4},{6,5},{7,6},{0,7},{9,8},{10,9},{11,1... | collective-permute-start | bytes 18440 | tf_op jit(solution)/shard_map/ppermute | solution.py:16
  72.0 1.4 copy-start.2
  72.7 5.4 %collective-permute-start.10 = (f32[64,1,384]{2,0,1:T(8,128)S(1)}, f32[64,1,384]{2,0,1:T(8,128)S(1)}, u32[]{:S(2)}, u32[]{:S(2)}) collective-permute-start(f32[64,1,384]{2,0,1:T(8,128)S(1)} %get-tuple-element.37), channel_id=1, source_target_pairs={{0,1},{1,2},{2,3},{3,4},{4,5},{5,6},{6,7},{7,0},{8,9},{9,10},{10,1... | collective-permute-start | bytes 294920 | tf_op jit(solution)/shard_map/ppermute | solution.py:13
  73.4 4.8 %collective-permute-start.11 = (f32[64,1,384]{2,0,1:T(8,128)S(1)}, f32[64,1,384]{2,0,1:T(8,128)S(1)}, u32[]{:S(2)}, u32[]{:S(2)}) collective-permute-start(f32[64,1,384]{2,0,1:T(8,128)S(1)} %get-tuple-element.38), channel_id=1, source_target_pairs={{1,0},{2,1},{3,2},{4,3},{5,4},{6,5},{7,6},{0,7},{9,8},{10,9},{11,1... | collective-permute-start | bytes 294920 | tf_op jit(solution)/shard_map/ppermute | solution.py:16
  82.0 5.5 %collective-permute-start.12 = (f32[64,1,384]{2,0,1:T(8,128)S(1)}, f32[64,1,384]{2,0,1:T(8,128)S(1)}, u32[]{:S(2)}, u32[]{:S(2)}) collective-permute-start(f32[64,1,384]{2,0,1:T(8,128)S(1)} %get-tuple-element.33), channel_id=1, source_target_pairs={{0,1},{1,2},{2,3},{3,4},{4,5},{5,6},{6,7},{7,0},{8,9},{9,10},{10,1... | collective-permute-start | bytes 294920 | tf_op jit(solution)/shard_map/ppermute | solution.py:13
  82.3 5.1 %collective-permute-start.13 = (f32[64,1,384]{2,0,1:T(8,128)S(1)}, f32[64,1,384]{2,0,1:T(8,128)S(1)}, u32[]{:S(2)}, u32[]{:S(2)}) collective-permute-start(f32[64,1,384]{2,0,1:T(8,128)S(1)} %get-tuple-element.34), channel_id=1, source_target_pairs={{1,0},{2,1},{3,2},{4,3},{5,4},{6,5},{7,6},{0,7},{9,8},{10,9},{11,1... | collective-permute-start | bytes 294920 | tf_op jit(solution)/shard_map/ppermute | solution.py:16
  92.7 6.5 %collective-permute-start.14 = (f32[64,1,384]{2,0,1:T(8,128)S(1)}, f32[64,1,384]{2,0,1:T(8,128)S(1)}, u32[]{:S(2)}, u32[]{:S(2)}) collective-permute-start(f32[64,1,384]{2,0,1:T(8,128)S(1)} %get-tuple-element.29), channel_id=1, source_target_pairs={{0,1},{1,2},{2,3},{3,4},{4,5},{5,6},{6,7},{7,0},{8,9},{9,10},{10,1... | collective-permute-start | bytes 294920 | tf_op jit(solution)/shard_map/ppermute | solution.py:13
  93.2 6.0 %collective-permute-start.15 = (f32[64,1,384]{2,0,1:T(8,128)S(1)}, f32[64,1,384]{2,0,1:T(8,128)S(1)}, u32[]{:S(2)}, u32[]{:S(2)}) collective-permute-start(f32[64,1,384]{2,0,1:T(8,128)S(1)} %get-tuple-element.30), channel_id=1, source_target_pairs={{1,0},{2,1},{3,2},{4,3},{5,4},{6,5},{7,6},{0,7},{9,8},{10,9},{11,1... | collective-permute-start | bytes 294920 | tf_op jit(solution)/shard_map/ppermute | solution.py:16
  105.2 6.5 %collective-permute-start.16 = (f32[64,1,384]{2,0,1:T(8,128)S(1)}, f32[64,1,384]{2,0,1:T(8,128)S(1)}, u32[]{:S(2)}, u32[]{:S(2)}) collective-permute-start(f32[64,1,384]{2,0,1:T(8,128)S(1)} %get-tuple-element.25), channel_id=1, source_target_pairs={{0,1},{1,2},{2,3},{3,4},{4,5},{5,6},{6,7},{7,0},{8,9},{9,10},{10,1... | collective-permute-start | bytes 294920 | tf_op jit(solution)/shard_map/ppermute | solution.py:13
  105.2 6.4 %collective-permute-start.17 = (f32[64,1,384]{2,0,1:T(8,128)S(1)}, f32[64,1,384]{2,0,1:T(8,128)S(1)}, u32[]{:S(2)}, u32[]{:S(2)}) collective-permute-start(f32[64,1,384]{2,0,1:T(8,128)S(1)} %get-tuple-element.26), channel_id=1, source_target_pairs={{1,0},{2,1},{3,2},{4,3},{5,4},{6,5},{7,6},{0,7},{9,8},{10,9},{11,1... | collective-permute-start | bytes 294920 | tf_op jit(solution)/shard_map/ppermute | solution.py:16
  117.5 6.5 %collective-permute-start.18 = (f32[64,1,384]{2,0,1:T(8,128)S(1)}, f32[64,1,384]{2,0,1:T(8,128)S(1)}, u32[]{:S(2)}, u32[]{:S(2)}) collective-permute-start(f32[64,1,384]{2,0,1:T(8,128)S(1)} %get-tuple-element.21), channel_id=1, source_target_pairs={{0,1},{1,2},{2,3},{3,4},{4,5},{5,6},{6,7},{7,0},{8,9},{9,10},{10,1... | collective-permute-start | bytes 294920 | tf_op jit(solution)/shard_map/ppermute | solution.py:13
  117.6 6.4 %collective-permute-start.19 = (f32[64,1,384]{2,0,1:T(8,128)S(1)}, f32[64,1,384]{2,0,1:T(8,128)S(1)}, u32[]{:S(2)}, u32[]{:S(2)}) collective-permute-start(f32[64,1,384]{2,0,1:T(8,128)S(1)} %get-tuple-element.22), channel_id=1, source_target_pairs={{1,0},{2,1},{3,2},{4,3},{5,4},{6,5},{7,6},{0,7},{9,8},{10,9},{11,1... | collective-permute-start | bytes 294920 | tf_op jit(solution)/shard_map/ppermute | solution.py:16
  124.0 5.8 %copy-start.3 = (bf16[6,64,64]{2,1,0:T(8,128)(2,1)S(1)}, bf16[6,64,64]{2,1,0:T(8,128)(2,1)}, u32[]{:S(2)}) copy-start(bf16[6,64,64]{2,1,0:T(8,128)(2,1)} %param.12) | copy-start | bytes 147460
  124.0 13.7 %copy-start.1 = (bf16[25,48,384]{2,1,0:T(8,128)(2,1)S(1)}, bf16[25,48,384]{2,1,0:T(8,128)(2,1)}, u32[]{:S(2)}) copy-start(bf16[25,48,384]{2,1,0:T(8,128)(2,1)} %param.7) | copy-start | bytes 2764804
Sparse Core Ops, SparseCore 0:
  8.9 33.1 all-gather.2
